TPU v7x, 32 devices: a whole 2x2x4 slice. The times are simulated.
32 devices in a mesh: seq: 8 (over z, x), vocab: 4 (over y, core).
Axes of the slice: x: 2, y: 2, z: 4, core: 2. Of those that a mesh axis runs over, the one named last changes fastest.
Arguments:
- hidden: bfloat16 [512, 4096], P('seq'), may hold values from -12 to 12
- head_weight: bfloat16 [4096, 126464], P(None, ('seq', 'vocab')), may hold values from -3 to 3
- teacher: bfloat16 [64, 126464], P(None, ('seq', 'vocab')), may hold values from -320 to 320
- positions: int32 [8, 8], P('seq'), may hold values from 0 to 63, as said below
- counts: int32 [8], P('seq'), may hold values from 1 to 8, 32 in all
Outputs:
- grad_hidden: bfloat16 [64, 4096], P(('seq', 'vocab'))
- grad_head: bfloat16 [4096, 126464], P(None, ('seq', 'vocab'))
Inputs may be any that keep to these rules, and one draw needn't show every extreme that they name: Each row holds 8 distinct token positions within its seq shard's block of 64 tokens; the first counts[s] of row s are its masked tokens. The counts sum to exactly 32.
All inputs are finite; a program needn't handle non-finite values. No bound on the sum of `counts` on one device may be relied on, other than what follows from the above.
Results may differ from a plain program's by a relative error of at most 0.012.
Values may be sent and summed in bfloat16 or wider, within the bound.
A program may use at most 128 MiB of HBM per device.

v0:
```python
import jax
import jax.numpy as jnp
from jax import lax
from jax.sharding import PartitionSpec as P

SPAN = 1


loss_scale = 1024.0


def per_device(hidden, head_weight, teacher, positions, counts):
    capacity = positions.shape[1]
    seq_devices = lax.axis_size("seq")
    picked = jnp.take(hidden, positions[0], axis=0)
    gathered, all_counts = (
        lax.all_gather(picked, "seq", axis=0, tiled=True),
        lax.all_gather(counts, "seq", axis=0, tiled=True),
    )
    slot_rank = jnp.arange(capacity, dtype=jnp.int32)[None, :]
    validity = (slot_rank < all_counts[:, None]).reshape(-1)
    seq_count = jnp.sum(all_counts.reshape(seq_devices // SPAN, SPAN), axis=1).astype(jnp.int32)
    per_slot = jnp.repeat(seq_count, SPAN * capacity)
    weight = jnp.where(validity, loss_scale / per_slot.astype(jnp.float32), 0.0)
    student = jnp.dot(gathered, head_weight, preferred_element_type=jnp.float32)
    teacher_full = teacher.astype(jnp.float32)
    top_student, top_teacher = lax.pmax(
        (jnp.max(student, axis=1), jnp.max(teacher_full, axis=1)), ("seq", "vocab")
    )
    total_student, total_teacher = lax.psum(
        (
            jnp.sum(jnp.exp(student - top_student[:, None]), axis=1),
            jnp.sum(jnp.exp(teacher_full - top_teacher[:, None]), axis=1),
        ),
        ("seq", "vocab"),
    )
    prob_student = jnp.exp(student - top_student[:, None]) / total_student[:, None]
    prob_teacher = jnp.exp(teacher_full - top_teacher[:, None]) / total_teacher[:, None]
    grad_logits = (weight[:, None] * (prob_student - prob_teacher)).astype(jnp.bfloat16)
    grad_head = lax.dot_general(
        gathered, grad_logits, (((0,), (0,)), ((), ())), preferred_element_type=jnp.float32
    ).astype(jnp.bfloat16)
    row_sum = lax.psum_scatter(
        lax.dot_general(
            grad_logits, head_weight, (((1,), (1,)), ((), ())), preferred_element_type=jnp.float32
        ),
        ("seq", "vocab"),
        scatter_dimension=0,
        tiled=True,
    )
    return (row_sum.astype(jnp.bfloat16), grad_head)


def solution(mesh):
    return jax.shard_map(
        per_device,
        mesh=mesh,
        in_specs=(
            P("seq", None),
            P(None, ("seq", "vocab")),
            P(None, ("seq", "vocab")),
            P("seq", None),
            P("seq"),
        ),
        out_specs=(P(("seq", "vocab"), None), P(None, ("seq", "vocab"))),
        check_vma=False,
    )
```

profile of v0, /device:TPU:0, one launch (start us, length us, event | category | flops | bytes accessed | tf_op | source)
XLA Modules:
  0.0 223.2 jit_solution(1681434097227076893)
XLA Ops:
  0.6 0.0 copy-start
  0.6 0.0 copy-start.1
  1.4 1.2 dynamic-slice
  2.6 0.7 fusion.3
  3.3 0.7 compare_and_fusion
  4.0 1.2 reduce_max.24
  5.2 0.8 dynamic-update-slice
  5.9 13.1 %all-reduce = s32[8]{0:T(128)S(1)} all-reduce(s32[8]{0:T(128)S(1)} %dynamic-update-slice), channel_id=1, replica_groups=mesh['seq'=8,'vocab'=4] {'seq'}, use_global_device_ids=true, to_apply=%add | all-reduce | flops 8 | bytes 64
  19.0 0.1 fusion.2
  19.1 0.1 select_n.32
  19.2 0.0 copy-done
  19.2 0.6 gather_fusion
  19.8 0.1 broadcast_select_fusion
  19.9 31.5 %all_gather.7 = bf16[64,4096]{1,0:T(8,128)(2,1)S(1)} all-gather(bf16[8,4096]{1,0:T(8,128)(2,1)S(1)} %broadcast_select_fusion), channel_id=1, replica_groups=mesh['seq'=8,'vocab'=4] {'seq'}, dimensions={0}, use_global_device_ids=true | all-gather | bytes 589824 | tf_op jit(solution)/shard_map/all_gather | solution.py:17
  51.4 14.9 %fusion.5 = (f32[64]{0:T(128)S(1)}, f32[64,3952]{1,0:T(8,128)S(1)}) fusion(bf16[64,4096]{1,0:T(8,128)(2,1)S(1)} %all_gather.7, bf16[4096,3952]{0,1:T(8,128)(2,1)} %param.6), kind=kOutput, calls=%fused_computation.18 | convolution fusion | flops 2072239104 | bytes 33911040 | tf_op jit(solution)/shard_map/dot_general | solution.py:25
  66.2 37.1 %all-reduce.3 = (f32[64]{0:T(128)S(1)}, f32[64]{0:T(128)S(1)}) all-reduce(bf16[64]{0:T(256)(128)(2,1)S(1)} %reduce_max.24, f32[64]{0:T(128)S(1)} %get-tuple-element.6), channel_id=1, replica_groups=mesh['seq'=8,'vocab'=4] {'seq','vocab'}, use_global_device_ids=true, to_apply=%region_5.6 | all-reduce | flops 128 | bytes 896 | tf_op jit(solution)/shard_map/pmax | solution.py:27
  103.3 0.0 copy-done.1
  103.3 0.5 fusion
  103.8 42.2 %all-reduce.2 = (f32[64]{0:T(128)S(1)}, f32[64]{0:T(128)S(1)}) all-reduce(f32[64]{0:T(128)S(1)} %get-tuple-element.8, f32[64]{0:T(128)S(1)} %get-tuple-element.9), channel_id=1, replica_groups=mesh['seq'=8,'vocab'=4] {'seq','vocab'}, use_global_device_ids=true, to_apply=%region_7.8 | all-reduce | flops 128 | bytes 1024 | tf_op jit(solution)/shard_map/psum | solution.py:30
  146.1 14.5 %fusion.4 = f32[64,4096]{1,0:T(8,128)} fusion(bf16[4096,3952]{0,1:T(8,128)(2,1)} %param.6, bf16[64,3952]{1,0:T(8,128)(2,1)S(1)} %copy-done.1, f32[64,3952]{1,0:T(8,128)S(1)} %get-tuple-element.7, f32[64]{0:T(128)S(1)} %get-tuple-element.2, f32[64]{0:T(128)S(1)} %get-tuple-element.4, f32[64]{0:T(128)S(1)} %get-tuple-element.3, f32[64]{0:T(128)S(1)} %get-tuple-element.5, ...), kind=kOutput, calls=%fused_computation.17 | convolution fusion | flops 2074009600 | bytes 34942208 | tf_op jit(solution)/shard_map/dot_general | solution.py:44
  160.5 47.9 %all-reduce.5 = bf16[64,4096]{1,0:T(8,128)(2,1)S(1)} all-reduce(f32[64,4096]{1,0:T(8,128)} %fusion.4), channel_id=2, replica_groups=mesh['seq'=8,'vocab'=4] {'seq','vocab'}, use_global_device_ids=true, to_apply=%region_8.9.clone | all-reduce | flops 262144 | bytes 1572864
  208.4 0.6 dynamic-slice_convert_fusion
  209.1 14.1 %convolution_convert_fusion = bf16[4096,3952]{0,1:T(8,128)(2,1)} fusion(bf16[64,4096]{1,0:T(8,128)(2,1)S(1)} %all_gather.7, bf16[64,3952]{1,0:T(8,128)(2,1)S(1)} %copy-done.1, f32[64,3952]{1,0:T(8,128)S(1)} %get-tuple-element.7, f32[64]{0:T(128)S(1)} %get-tuple-element.2, f32[64]{0:T(128)S(1)} %get-tuple-element.4, f32[64]{0:T(128)S(1)} %get-tuple-element.3, ...), kind=kOutput, calls=%fused_computation.1 | convolution fusion | flops 2090196992 | bytes 34417920 | tf_op jit(solution)/shard_map/dot_general | solution.py:40
  (3 shorter events, 0.0 us)
Async XLA Ops:
  0.6 18.5 %copy-start = (bf16[64,4096]{1,0:T(8,128)(2,1)S(1)}, bf16[64,4096]{1,0:T(8,128)(2,1)}, u32[]{:S(2)}) copy-start(bf16[64,4096]{1,0:T(8,128)(2,1)} %param.5) | copy-start | bytes 1572868
  0.6 102.7 %copy-start.1 = (bf16[64,3952]{1,0:T(8,128)(2,1)S(1)}, bf16[64,3952]{1,0:T(8,128)(2,1)}, u32[]{:S(2)}) copy-start(bf16[64,3952]{1,0:T(8,128)(2,1)} %param.7) | copy-start | bytes 1517572
where the time goes:
time: 224 us; the launch traced here: 223 us
  blocking collectives  172 us (77%)
  matrix products  43.4 us (19%)
  local copies, waits for them, and re-layouts  3.32 us (1%)
  other arithmetic  3.16 us (1%)
    unnamed x2, blocking collectives  61 us
    psum x1, blocking collectives, per_device(): lax.psum((jnp.sum(jnp.exp(student - top_student[:, None]), axis=1), jnp.s...  42.2 us
    pmax x1, blocking collectives, per_device(): lax.pmax((jnp.max(student, axis=1), jnp.max(teacher_full, axis=1)), ('seq...  37.1 us
    all_gather x1, blocking collectives, per_device(): lax.all_gather(picked, 'seq', axis=0, tiled=True)  31.5 us
    dot_general x1, matrix products, per_device(): student = jnp.dot(gathered, head_weight, preferred_element_type=jnp.float32)  14.9 us
    dot_general x1, matrix products, per_device(): lax.dot_general(grad_logits, head_weight, (((1,), (1,)), ((), ())), prefe...  14.5 us
    dot_general x1, matrix products, per_device(): lax.dot_general(gathered, grad_logits, (((0,), (0,)), ((), ())), preferre...  14.1 us

commit v1 on v0

v1 whole, which is shorter than its diff:
```python
import functools

import jax
import jax.numpy as jnp
from jax import lax
from jax.experimental import pallas as pl
from jax.experimental.pallas import tpu as pltpu
from jax.sharding import PartitionSpec as P

MESH = pl.DeviceIdType.MESH
LOSS_SCALE = 1024.0
F32 = jnp.float32
BF16 = jnp.bfloat16


def chunks_of(size, step):
    if size % 16:
        return 0, 0, size
    full = size // step
    return full, full * step, size - full * step


def front_kernel(
    n_seq, n_voc, step,
    pos_ref, cnt_ref, hid_ref, tea_ref, w_hbm,
    picked_ref, grad_ref, gh_ref,
    w_ref, gb, picked, stu, tex, grad, st1, st2, xs, xr, bs, br, cg, gh32,
    w_sem, g1s, g1r, g2s, g2r, s1s, s1r, s2s, s2r, as_, ar, bss, bsr, cs, cr,
):
    slots, vocab = tea_ref.shape
    depth = hid_ref.shape[1]
    cap = pos_ref.shape[1]
    half = depth // 2
    quart = depth // 4
    own_cols = depth // n_voc
    sub = own_cols // 2
    halves = n_voc // 2
    group = n_seq * halves
    lanes = st1.shape[2]
    s = lax.axis_index("seq")
    v = lax.axis_index("vocab")
    core = v % 2
    other = 1 - core
    pair = v + 1 - 2 * core
    hv = v // 2
    flat = s * halves + hv
    full, tail_at, tail = chunks_of(vocab, step)

    def w_copy(i):
        rows = pl.ds(pl.multiple_of(i * step, step), step)
        return pltpu.make_async_copy(w_hbm.at[rows], w_ref.at[rows], w_sem.at[i])

    def w_tail():
        if full == 0:
            return pltpu.make_async_copy(w_hbm, w_ref, w_sem.at[0])
        rows = pl.ds(tail_at, tail)
        return pltpu.make_async_copy(w_hbm.at[rows], w_ref.at[rows], w_sem.at[full])

    if full:
        @pl.loop(0, full)
        def _(i):
            w_copy(i).start()
    if tail:
        w_tail().start()

    barrier = pltpu.get_barrier_semaphore()

    @pl.loop(1, group)
    def _(k):
        to = (flat + k) % group
        pl.semaphore_signal(
            barrier, inc=1, device_id=(to // halves, 2 * (to % halves) + core), device_id_type=MESH
        )

    @pl.loop(0, halves)
    def _(k):
        pl.semaphore_signal(barrier, inc=1, device_id=(s, 2 * k + other), device_id_type=MESH)

    tokens = hid_ref.shape[0]
    at_row = lax.broadcasted_iota(jnp.int32, (cap, tokens), 0)
    at_tok = lax.broadcasted_iota(jnp.int32, (cap, tokens), 1)
    hot = jnp.zeros((cap, tokens), F32)
    for k in range(cap):
        hot = jnp.where((at_row == k) & (at_tok == pos_ref[0, k]), 1.0, hot)
    mine = jnp.dot(hot.astype(BF16), hid_ref[...], preferred_element_type=F32)
    for h in range(2):
        lo = mine[:, h * half : h * half + quart]
        hi = mine[:, h * half + quart : (h + 1) * half]
        gb[s, h] = jnp.concatenate([lo, hi], axis=0).astype(BF16)

    pl.semaphore_wait(barrier, group - 1 + halves)

    def gather1(k, frm):
        return pltpu.make_async_remote_copy(
            src_ref=gb.at[frm, core], dst_ref=gb.at[frm, core],
            send_sem=g1s.at[k], recv_sem=g1r.at[frm],
            device_id=((s + k) % n_seq, v), device_id_type=MESH,
        )

    def gather2(frm, col):
        return pltpu.make_async_remote_copy(
            src_ref=gb.at[frm, col], dst_ref=gb.at[frm, col],
            send_sem=g2s.at[frm], recv_sem=g2r.at[frm],
            device_id=(s, pair), device_id_type=MESH,
        )

    @pl.loop(1, n_seq)
    def _(k):
        gather1(k, s).start()

    def over(body, init):
        carry = init
        if full:
            carry = lax.fori_loop(
                0, full, lambda i, c: body(pl.ds(pl.multiple_of(i * step, step), step), c), carry
            )
        if tail:
            carry = body(pl.ds(tail_at, tail), carry)
        return carry

    low = jnp.full((slots, 1), -jnp.inf, F32)
    none = jnp.zeros((slots, 1), F32)
    top_t = over(
        lambda at, c: jnp.maximum(c, jnp.max(tea_ref[:, at].astype(F32), axis=1, keepdims=True)), low
    )

    def teacher_total(at, c):
        e = jnp.exp(tea_ref[:, at].astype(F32) - top_t)
        tex[:, at] = e
        return c + jnp.sum(e, axis=1, keepdims=True)

    tot_t = over(teacher_total, none)

    @pl.loop(1, n_seq)
    def _(k):
        frm = (s + n_seq - k) % n_seq
        gather1(k, frm).wait_recv()
        gather2(frm, core).start()

    @pl.loop(1, n_seq)
    def _(k):
        gather2((s + n_seq - k) % n_seq, other).wait_recv()

    @pl.loop(0, n_seq // 2)
    def _(i):
        rows = pl.ds(pl.multiple_of(i * 2 * cap, 2 * cap), 2 * cap)
        for h in range(2):
            a = gb[2 * i, h].astype(F32)
            b = gb[2 * i + 1, h].astype(F32)
            for j in range(2):
                both = jnp.concatenate([a[j * cap : (j + 1) * cap], b[j * cap : (j + 1) * cap]], axis=0)
                picked[rows, h * half + j * quart : h * half + (j + 1) * quart] = both.astype(BF16)

    picked_ref[...] = picked[...]

    def student(at, top):
        block = lax.dot_general(
            w_ref[at, :], picked[...], (((1,), (1,)), ((), ())), preferred_element_type=F32
        )
        block = block.T
        stu[:, at] = block
        return jnp.maximum(top, jnp.max(block, axis=1, keepdims=True))

    top_s = low
    if full:
        def student_step(i, top):
            w_copy(i).wait()
            return student(pl.ds(pl.multiple_of(i * step, step), step), top)

        top_s = lax.fori_loop(0, full, student_step, top_s)
    if tail:
        w_tail().wait()
        top_s = student(pl.ds(tail_at, tail), top_s)

    def student_total(at, c):
        e = jnp.exp(stu[:, at] - top_s)
        stu[:, at] = e
        return c + jnp.sum(e, axis=1, keepdims=True)

    tot_s = over(student_total, none)

    lane = lax.broadcasted_iota(jnp.int32, (slots, 128), 1)
    wide = jnp.where(lane == 0, top_s, jnp.where(lane == 1, tot_s, jnp.where(lane == 2, top_t, tot_t)))
    if lanes > slots:
        wide = jnp.concatenate([wide, jnp.zeros((lanes - slots, 128), F32)], axis=0)
    st1[v] = wide.T[0:8, :]

    def stats1(k, frm):
        return pltpu.make_async_remote_copy(
            src_ref=st1.at[frm], dst_ref=st1.at[frm],
            send_sem=s1s.at[k], recv_sem=s1r.at[frm],
            device_id=(s, (v + k) % n_voc), device_id_type=MESH,
        )

    def stats2(k, frm):
        return pltpu.make_async_remote_copy(
            src_ref=st2.at[frm], dst_ref=st2.at[frm],
            send_sem=s2s.at[k], recv_sem=s2r.at[frm],
            device_id=((s + k) % n_seq, v), device_id_type=MESH,
        )

    def merge(ref):
        x = ref[...]
        ms, zs, mt, zt = x[:, 0:1, :], x[:, 1:2, :], x[:, 2:3, :], x[:, 3:4, :]
        top1 = jnp.max(ms, axis=0)
        top2 = jnp.max(mt, axis=0)
        return (
            top1, jnp.sum(zs * jnp.exp(ms - top1[None]), axis=0),
            top2, jnp.sum(zt * jnp.exp(mt - top2[None]), axis=0),
            jnp.sum(x[:, 4:5, :], axis=0),
        )

    for k in range(1, n_voc):
        stats1(k, v).start()
    for k in range(1, n_voc):
        stats1(k, (v + n_voc - k) % n_voc).wait_recv()
    slot_lane = lax.broadcasted_iota(jnp.int32, (1, lanes), 1)
    count = cnt_ref[0].astype(F32)
    my_count = jnp.where(slot_lane // cap == s, count, 0.0)
    m1, z1, m2, z2, _ = merge(st1)
    st2[s] = jnp.concatenate([m1, z1, m2, z2, my_count, jnp.zeros((3, lanes), F32)], axis=0)

    @pl.loop(1, n_seq)
    def _(k):
        stats2(k, s).start()

    @pl.loop(1, n_seq)
    def _(k):
        stats2(k, (s + n_seq - k) % n_seq).wait_recv()

    m1, z1, m2, z2, counts = merge(st2)
    weight = jnp.where(
        (slot_lane % cap).astype(F32) < counts, LOSS_SCALE / jnp.maximum(counts, 1.0), 0.0
    )
    rows = jnp.concatenate([m1, weight / z1, m2, weight / z2, jnp.zeros((124, lanes), F32)], axis=0)
    cols = rows.T[0:slots]
    scale_s = cols[:, 1:2] * jnp.exp(top_s - cols[:, 0:1])
    scale_t = cols[:, 3:4] * jnp.exp(top_t - cols[:, 2:3])

    def logits(at, c):
        grad[:, at] = (scale_s * stu[:, at] - scale_t * tex[:, at]).astype(BF16)
        return c

    over(logits, 0)
    grad_ref[...] = grad[...]

    def part(q, store):
        @pl.loop(0, 2)
        def _(j):
            at = pl.ds(pl.multiple_of(q * own_cols + j * sub, sub), sub)
            store(j, jnp.dot(grad[...], w_ref[:, at], preferred_element_type=F32))

    def to_pair(i):
        return pltpu.make_async_remote_copy(
            src_ref=xs.at[i], dst_ref=xr.at[i], send_sem=as_.at[i], recv_sem=ar.at[i],
            device_id=(s, pair), device_id_type=MESH,
        )

    def to_owner(i, k):
        h = (hv + 1 + i) % halves
        seq = (s + k) % n_seq
        return pltpu.make_async_remote_copy(
            src_ref=bs.at[i, seq], dst_ref=br.at[flat],
            send_sem=bss.at[i, k], recv_sem=bsr.at[flat],
            device_id=(seq, 2 * h + core), device_id_type=MESH,
        )

    for i in range(halves):
        h = (hv + 1 + i) % halves

        def store_pair(j, value, i=i):
            xs[i, j] = value

        part(2 * h + other, store_pair)
        to_pair(i).start()

        def store_own(j, value, i=i):
            for q in range(n_seq):
                bs32 = value[q * cap : (q + 1) * cap]
                gh32[q, pl.ds(pl.multiple_of(j * cap, cap), cap), :] = bs32

        part(2 * h + core, store_own)
        to_pair(i).wait_recv()
        for q in range(n_seq):
            for_q = [xr[i, j, q * cap : (q + 1) * cap, :] for j in range(2)]
            bs[i, q] = (gh32[q] + jnp.concatenate(for_q, axis=0)).astype(BF16)
        last = i == halves - 1
        for k in range(1 if last else 0, n_seq):
            to_owner(i, k).start()

    br[flat] = bs[halves - 1, s]

    def got(k):
        frm = (flat + k) % group
        return pltpu.make_async_remote_copy(
            src_ref=bs.at[0, 0], dst_ref=br.at[frm],
            send_sem=bss.at[0, 0], recv_sem=bsr.at[frm],
            device_id=(frm // halves, 2 * (frm % halves) + core), device_id_type=MESH,
        )

    @pl.loop(1, group)
    def _(k):
        got(k).wait_recv()

    total = lax.fori_loop(
        0, group, lambda k, c: c + br[k].astype(F32), jnp.zeros((2 * cap, sub), F32)
    )
    cg[v] = total.astype(BF16)

    def to_row(k, frm):
        return pltpu.make_async_remote_copy(
            src_ref=cg.at[frm], dst_ref=cg.at[frm], send_sem=cs.at[k], recv_sem=cr.at[frm],
            device_id=(s, (v + k) % n_voc), device_id_type=MESH,
        )

    for k in range(1, n_voc):
        to_row(k, v).start()
    for k in range(1, n_voc):
        to_row(k, (v + n_voc - k) % n_voc).wait_recv()
    per = cap // n_voc
    row_at = lax.broadcasted_iota(jnp.int32, (cap, sub), 0)
    for r in range(per):
        for q in range(n_voc):
            both = cg[q].astype(F32)
            for j in range(2):
                row = jnp.sum(
                    jnp.where(row_at == per * v + r, both[j * cap : (j + 1) * cap], 0.0),
                    axis=0, keepdims=True,
                )
                gh_ref[r : r + 1, q * own_cols + j * sub : q * own_cols + (j + 1) * sub] = row

    @pl.loop(1, n_seq)
    def _(k):
        gather1(k, s).wait_send()
        gather2((s + n_seq - k) % n_seq, core).wait_send()
        stats2(k, s).wait_send()

    for k in range(1, n_voc):
        stats1(k, v).wait_send()
        to_row(k, v).wait_send()
    for i in range(halves):
        to_pair(i).wait_send()
        for k in range(1 if i == halves - 1 else 0, n_seq):
            to_owner(i, k).wait_send()


def head_kernel(g_ref, p_ref, out_ref):
    out_ref[...] = lax.dot_general(
        g_ref[...], p_ref[...], (((0,), (0,)), ((), ())), preferred_element_type=F32
    ).astype(BF16)


def per_device(n_seq, n_voc, hidden, head_weight, teacher, positions, counts):
    slots, vocab = teacher.shape
    depth = hidden.shape[1]
    cap = positions.shape[1]
    halves = n_voc // 2
    group = n_seq * halves
    sub = depth // n_voc // 2
    lanes = -(-slots // 128) * 128
    step = 512
    n_chunks = chunks_of(vocab, step)[0] + 1
    vmem = pl.BlockSpec(memory_space=pltpu.VMEM)
    smem = pl.BlockSpec(memory_space=pltpu.SMEM)
    dma = pltpu.SemaphoreType.DMA
    picked, grad, gh = pl.pallas_call(
        functools.partial(front_kernel, n_seq, n_voc, step),
        out_shape=(
            jax.ShapeDtypeStruct((slots, depth), BF16),
            jax.ShapeDtypeStruct((slots, vocab), BF16),
            jax.ShapeDtypeStruct((cap // n_voc, depth), F32),
        ),
        in_specs=[smem, smem, vmem, vmem, pl.BlockSpec(memory_space=pl.ANY)],
        out_specs=(vmem, vmem, vmem),
        scratch_shapes=[
            pltpu.VMEM((vocab, depth), BF16),
            pltpu.VMEM((n_seq, 2, 2 * cap, depth // 4), BF16),
            pltpu.VMEM((slots, depth), BF16),
            pltpu.VMEM((slots, vocab), F32),
            pltpu.VMEM((slots, vocab), F32),
            pltpu.VMEM((slots, vocab), BF16),
            pltpu.VMEM((n_voc, 8, lanes), F32),
            pltpu.VMEM((n_seq, 8, lanes), F32),
            pltpu.VMEM((halves, 2, slots, sub), F32),
            pltpu.VMEM((halves, 2, slots, sub), F32),
            pltpu.VMEM((halves, n_seq, 2 * cap, sub), BF16),
            pltpu.VMEM((group, 2 * cap, sub), BF16),
            pltpu.VMEM((n_voc, 2 * cap, sub), BF16),
            pltpu.VMEM((n_seq, 2 * cap, sub), F32),
            dma((n_chunks,)),
            dma((n_seq,)), dma((n_seq,)), dma((n_seq,)), dma((n_seq,)),
            dma((n_voc,)), dma((n_voc,)), dma((n_seq,)), dma((n_seq,)),
            dma((halves,)), dma((halves,)),
            dma((halves, n_seq)), dma((group,)),
            dma((n_voc,)), dma((n_voc,)),
        ],
        compiler_params=pltpu.CompilerParams(
            collective_id=0, has_side_effects=True, vmem_limit_bytes=54 * 1024 * 1024
        ),
        cost_estimate=pl.CostEstimate(
            flops=4 * slots * depth * vocab, bytes_accessed=2 * depth * vocab, transcendentals=2 * slots * vocab
        ),
        name="front",
    )(positions, counts, hidden, teacher, head_weight.T)

    rows = 256
    head = pl.pallas_call(
        head_kernel,
        out_shape=jax.ShapeDtypeStruct((vocab, depth), BF16),
        grid=(pl.cdiv(vocab, rows),),
        in_specs=[
            pl.BlockSpec((slots, rows), lambda i: (0, i)),
            pl.BlockSpec((slots, depth), lambda i: (0, 0)),
        ],
        out_specs=pl.BlockSpec((rows, depth), lambda i: (i, 0)),
        compiler_params=pltpu.CompilerParams(vmem_limit_bytes=40 * 1024 * 1024),
        cost_estimate=pl.CostEstimate(
            flops=2 * slots * depth * vocab, bytes_accessed=2 * depth * vocab, transcendentals=0
        ),
        name="head",
    )(grad, picked)
    return gh.astype(BF16), head.T


def solution(mesh):
    return jax.shard_map(
        functools.partial(per_device, mesh.shape["seq"], mesh.shape["vocab"]),
        mesh=mesh,
        in_specs=(
            P("seq", None),
            P(None, ("seq", "vocab")),
            P(None, ("seq", "vocab")),
            P("seq", None),
            P("seq"),
        ),
        out_specs=(P(("seq", "vocab"), None), P(None, ("seq", "vocab"))),
        check_vma=False,
    )
```

time: 224 us -> 72.4 us (0.32)
  blocking collectives: 172 us -> 0 us
  Pallas kernels: 0 us -> 67.3 us
  matrix products: 43.4 us -> 0 us
    pallas_call x0 -> x2, Pallas kernels: none -> 67.3 us  [the longest x1 50.6 us: per_device(): pl.pallas_call(functools.partial(front_kernel, n_seq, n_voc, step), out_s...]
    unnamed x2 -> x0, blocking collectives: 61 us -> none
    dot_general x3 -> x0, matrix products: 43.4 us -> none  [the longest x1 14.9 us: per_device(): student = jnp.dot(gathered, head_weight, preferred_element_type=jnp.float32)]
    psum x1 -> x0, blocking collectives: 42.2 us -> none  [per_device(): lax.psum((jnp.sum(jnp.exp(student - top_student[:, None]), axis=1), jnp.s...]
    pmax x1 -> x0, blocking collectives: 37.1 us -> none  [per_device(): lax.pmax((jnp.max(student, axis=1), jnp.max(teacher_full, axis=1)), ('seq...]
    all_gather x1 -> x0, blocking collectives: 31.5 us -> none  [per_device(): lax.all_gather(picked, 'seq', axis=0, tiled=True)]
where the time goes in v1:
time: 72.4 us; the launch traced here: 72.1 us
  Pallas kernels  67.3 us (93%)
  local copies, waits for them, and re-layouts  2.08 us (3%)
  other arithmetic  1.38 us (2%)
  between operations  1.29 us (2%)
    pallas_call x1, Pallas kernels, per_device(): pl.pallas_call(functools.partial(front_kernel, n_seq, n_voc, step), out_s...  50.6 us
    pallas_call x1, Pallas kernels, per_device(): pl.pallas_call(head_kernel, out_shape=jax.ShapeDtypeStruct((vocab, depth)...  16.8 us
    unnamed x4, local copies, waits for them, and re-layouts  2.08 us

profile of v1, /device:TPU:0, one launch (start us, length us, event | category | flops | bytes accessed | tf_op | source)
XLA Modules:
  0.0 72.1 jit_solution(16182542215464719816)
XLA Ops:
  1.3 50.6 %front.1 = (bf16[64,4096]{1,0:T(8,128)(2,1)}, bf16[64,3952]{1,0:T(8,128)(2,1)}, f32[2,4096]{1,0:T(2,128)}) custom-call(s32[1,8]{1,0:T(1,128)} %pos_ref.1, s32[1]{0:T(128)S(6)} %copy.7.cnt_ref, bf16[64,4096]{1,0:T(8,128)(2,1)} %hid_ref.1, bf16[64,3952]{1,0:T(8,128)(2,1)} %tea_ref.1, bf16[3952,4096]{1,0:T(8,128)(2,1)} %bitcast.2), custom_call_target="tpu_custom_call" | custom-call | flops 4143972352 | bytes 32374784 | tf_op jit(solution)/shard_map/front/pallas_call | solution.py:366
  51.8 1.4 %convert_element_type.3 = bf16[2,4096]{1,0:T(2,128)(2,1)} convert(f32[2,4096]{1,0:T(2,128)} %get-tuple-element.5) | non-fusion elementwise | flops 8192 | bytes 49152 | tf_op jit(solution)/shard_map/convert_element_type | solution.py:422
  53.2 0.0 copy-start
  53.2 1.0 %copy-done = bf16[64,4096]{1,0:T(8,128)(2,1)S(1)} copy-done((bf16[64,4096]{1,0:T(8,128)(2,1)S(1)}, bf16[64,4096]{1,0:T(8,128)(2,1)}, u32[]{:S(2)}) %copy-start) | copy-done | bytes 524312
  54.3 0.0 copy-start.1
  54.3 1.0 %copy-done.1 = bf16[64,3952]{1,0:T(8,128)(2,1)S(1)} copy-done((bf16[64,3952]{1,0:T(8,128)(2,1)S(1)}, bf16[64,3952]{1,0:T(8,128)(2,1)}, u32[]{:S(2)}) %copy-start.1) | copy-done | bytes 505880
  55.3 16.8 %head.1 = bf16[3952,4096]{1,0:T(8,128)(2,1)} custom-call(bf16[64,3952]{1,0:T(8,128)(2,1)S(1)} %copy-done.1, bf16[64,4096]{1,0:T(8,128)(2,1)S(1)} %copy-done), custom_call_target="tpu_custom_call" | custom-call | flops 2071986176 | bytes 32374784 | tf_op jit(solution)/shard_map/head/pallas_call | solution.py:407
Async XLA Ops:
  53.2 1.0 %copy-start = (bf16[64,4096]{1,0:T(8,128)(2,1)S(1)}, bf16[64,4096]{1,0:T(8,128)(2,1)}, u32[]{:S(2)}) copy-start(bf16[64,4096]{1,0:T(8,128)(2,1)} %get-tuple-element.7.p_ref) | copy-start | bytes 1572868
  54.3 1.0 %copy-start.1 = (bf16[64,3952]{1,0:T(8,128)(2,1)S(1)}, bf16[64,3952]{1,0:T(8,128)(2,1)}, u32[]{:S(2)}) copy-start(bf16[64,3952]{1,0:T(8,128)(2,1)} %get-tuple-element.6.g_ref) | copy-start | bytes 1517572

commit v2 on v1

--- a/solution.py
+++ b/solution.py
@@ -25,7 +25,7 @@
     pos_ref, cnt_ref, hid_ref, tea_ref, w_hbm,
     picked_ref, grad_ref, gh_ref,
     w_ref, gb, picked, stu, tex, grad, st1, st2, xs, xr, bs, br, cg, gh32,
-    w_sem, g1s, g1r, g2s, g2r, s1s, s1r, s2s, s2r, as_, ar, bss, bsr, cs, cr,
+    w_sem, g1s, g1r, g2s, g2r, s1s, s1r, s2s, s2r, as_, ar, bss, bsr, cs, cr, out_sem,
 ):
     slots, vocab = tea_ref.shape
     depth = hid_ref.shape[1]
@@ -151,7 +151,8 @@
                 both = jnp.concatenate([a[j * cap : (j + 1) * cap], b[j * cap : (j + 1) * cap]], axis=0)
                 picked[rows, h * half + j * quart : h * half + (j + 1) * quart] = both.astype(BF16)
 
-    picked_ref[...] = picked[...]
+    picked_out = pltpu.make_async_copy(picked, picked_ref, out_sem.at[0])
+    picked_out.start()
 
     def student(at, top):
         block = lax.dot_general(
@@ -242,7 +243,8 @@
         return c
 
     over(logits, 0)
-    grad_ref[...] = grad[...]
+    grad_out = pltpu.make_async_copy(grad, grad_ref, out_sem.at[1])
+    grad_out.start()
 
     def part(q, store):
         @pl.loop(0, 2)
@@ -329,6 +331,8 @@
                 )
                 gh_ref[r : r + 1, q * own_cols + j * sub : q * own_cols + (j + 1) * sub] = row
 
+    picked_out.wait()
+    grad_out.wait()
     @pl.loop(1, n_seq)
     def _(k):
         gather1(k, s).wait_send()
@@ -344,10 +348,50 @@
             to_owner(i, k).wait_send()
 
 
-def head_kernel(g_ref, p_ref, out_ref):
-    out_ref[...] = lax.dot_general(
-        g_ref[...], p_ref[...], (((0,), (0,)), ((), ())), preferred_element_type=F32
-    ).astype(BF16)
+def head_kernel(
+    step, g_hbm, p_hbm, gh32_hbm, out_hbm, gh_ref, g_ref, p_ref, gh32_ref, buf, sem, in_sem
+):
+    taken = [
+        pltpu.make_async_copy(src, dst, in_sem.at[i])
+        for i, (src, dst) in enumerate(((g_hbm, g_ref), (p_hbm, p_ref), (gh32_hbm, gh32_ref)))
+    ]
+    for one in taken:
+        one.start()
+    for one in taken:
+        one.wait()
+    gh_ref[...] = gh32_ref[...].astype(BF16)
+    vocab = g_ref.shape[1]
+    full, tail_at, tail = chunks_of(vocab, step)
+
+    def fill(at):
+        buf[at, :] = lax.dot_general(
+            g_ref[:, at], p_ref[...], (((0,), (0,)), ((), ())), preferred_element_type=F32
+        ).astype(BF16)
+
+    def copy(i):
+        rows = pl.ds(pl.multiple_of(i * step, step), step)
+        return pltpu.make_async_copy(buf.at[rows], out_hbm.at[rows], sem.at[i])
+
+    def copy_tail():
+        if full == 0:
+            return pltpu.make_async_copy(buf, out_hbm, sem.at[0])
+        rows = pl.ds(tail_at, tail)
+        return pltpu.make_async_copy(buf.at[rows], out_hbm.at[rows], sem.at[full])
+
+    if full:
+        @pl.loop(0, full)
+        def _(i):
+            fill(pl.ds(pl.multiple_of(i * step, step), step))
+            copy(i).start()
+    if tail:
+        fill(pl.ds(tail_at, tail))
+        copy_tail().start()
+    if full:
+        @pl.loop(0, full)
+        def _(i):
+            copy(i).wait()
+    if tail:
+        copy_tail().wait()
 
 
 def per_device(n_seq, n_voc, hidden, head_weight, teacher, positions, counts):
@@ -358,10 +402,11 @@
     group = n_seq * halves
     sub = depth // n_voc // 2
     lanes = -(-slots // 128) * 128
-    step = 512
+    step = 1024
     n_chunks = chunks_of(vocab, step)[0] + 1
     vmem = pl.BlockSpec(memory_space=pltpu.VMEM)
     smem = pl.BlockSpec(memory_space=pltpu.SMEM)
+    anywhere = pl.BlockSpec(memory_space=pl.ANY)
     dma = pltpu.SemaphoreType.DMA
     picked, grad, gh = pl.pallas_call(
         functools.partial(front_kernel, n_seq, n_voc, step),
@@ -371,7 +416,7 @@
             jax.ShapeDtypeStruct((cap // n_voc, depth), F32),
         ),
         in_specs=[smem, smem, vmem, vmem, pl.BlockSpec(memory_space=pl.ANY)],
-        out_specs=(vmem, vmem, vmem),
+        out_specs=(anywhere, anywhere, vmem),
         scratch_shapes=[
             pltpu.VMEM((vocab, depth), BF16),
             pltpu.VMEM((n_seq, 2, 2 * cap, depth // 4), BF16),
@@ -392,7 +437,7 @@
             dma((n_voc,)), dma((n_voc,)), dma((n_seq,)), dma((n_seq,)),
             dma((halves,)), dma((halves,)),
             dma((halves, n_seq)), dma((group,)),
-            dma((n_voc,)), dma((n_voc,)),
+            dma((n_voc,)), dma((n_voc,)), dma((2,)),
         ],
         compiler_params=pltpu.CompilerParams(
             collective_id=0, has_side_effects=True, vmem_limit_bytes=54 * 1024 * 1024
@@ -403,23 +448,30 @@
         name="front",
     )(positions, counts, hidden, teacher, head_weight.T)
 
-    rows = 256
-    head = pl.pallas_call(
-        head_kernel,
-        out_shape=jax.ShapeDtypeStruct((vocab, depth), BF16),
-        grid=(pl.cdiv(vocab, rows),),
-        in_specs=[
-            pl.BlockSpec((slots, rows), lambda i: (0, i)),
-            pl.BlockSpec((slots, depth), lambda i: (0, 0)),
+    rows = 512
+    head, gh = pl.pallas_call(
+        functools.partial(head_kernel, rows),
+        out_shape=(
+            jax.ShapeDtypeStruct((vocab, depth), BF16),
+            jax.ShapeDtypeStruct((cap // n_voc, depth), BF16),
+        ),
+        in_specs=[anywhere, anywhere, anywhere],
+        out_specs=(anywhere, vmem),
+        scratch_shapes=[
+            pltpu.VMEM((slots, vocab), BF16),
+            pltpu.VMEM((slots, depth), BF16),
+            pltpu.VMEM((cap // n_voc, depth), F32),
+            pltpu.VMEM((vocab, depth), BF16),
+            dma((chunks_of(vocab, rows)[0] + 1,)),
+            dma((3,)),
         ],
-        out_specs=pl.BlockSpec((rows, depth), lambda i: (i, 0)),
-        compiler_params=pltpu.CompilerParams(vmem_limit_bytes=40 * 1024 * 1024),
+        compiler_params=pltpu.CompilerParams(vmem_limit_bytes=48 * 1024 * 1024),
         cost_estimate=pl.CostEstimate(
             flops=2 * slots * depth * vocab, bytes_accessed=2 * depth * vocab, transcendentals=0
         ),
         name="head",
-    )(grad, picked)
-    return gh.astype(BF16), head.T
+    )(grad, picked, gh)
+    return gh, head.T
 
 
 def solution(mesh):

time: 72.4 us -> 65.8 us (0.909)
  Pallas kernels: 67.3 us -> 61.4 us
  other arithmetic: 1.38 us -> 0 us
  local copies, waits for them, and re-layouts: 2.08 us -> 2.83 us
    pallas_call x1, Pallas kernels: 16.8 us -> 13 us  [per_device(): pl.pallas_call(functools.partial(head_kernel, rows), out_shape=(jax.Shape...]
    pallas_call x1, Pallas kernels: 50.6 us -> 48.4 us  [per_device(): pl.pallas_call(functools.partial(front_kernel, n_seq, n_voc, step), out_s...]
    convert_element_type x1 -> x0, other arithmetic: 1.38 us -> none  [per_device(): return (gh.astype(BF16), head.T)]
    unnamed x4 -> x6, local copies, waits for them, and re-layouts: 2.08 us -> 2.83 us
where the time goes in v2:
time: 65.8 us; the launch traced here: 65.5 us
  Pallas kernels  61.4 us (93%)
  local copies, waits for them, and re-layouts  2.83 us (4%)
  between operations  1.3 us (2%)
    pallas_call x1, Pallas kernels, per_device(): pl.pallas_call(functools.partial(front_kernel, n_seq, n_voc, step), out_s...  48.4 us
    pallas_call x1, Pallas kernels, per_device(): pl.pallas_call(functools.partial(head_kernel, rows), out_shape=(jax.Shape...  13 us
    unnamed x6, local copies, waits for them, and re-layouts  2.83 us

profile of v2, /device:TPU:0, one launch (start us, length us, event | category | flops | bytes accessed | tf_op | source)
XLA Modules:
  0.0 65.5 jit_solution(5981297212784210798)
XLA Ops:
  1.3 48.4 %front.1 = (bf16[64,4096]{1,0:T(8,128)(2,1)}, bf16[64,3952]{1,0:T(8,128)(2,1)}, f32[2,4096]{1,0:T(2,128)}) custom-call(s32[1,8]{1,0:T(1,128)} %pos_ref.1, s32[1]{0:T(128)S(6)} %copy.7.cnt_ref, bf16[64,4096]{1,0:T(8,128)(2,1)} %hid_ref.1, bf16[64,3952]{1,0:T(8,128)(2,1)} %tea_ref.1, bf16[3952,4096]{1,0:T(8,128)(2,1)} %bitcast.2), custom_call_target="tpu_custom_call" | custom-call | flops 4143972352 | bytes 32374784 | tf_op jit(solution)/shard_map/front/pallas_call | solution.py:411
  49.7 0.0 copy-start
  49.7 1.0 %copy-done = bf16[64,4096]{1,0:T(8,128)(2,1)S(1)} copy-done((bf16[64,4096]{1,0:T(8,128)(2,1)S(1)}, bf16[64,4096]{1,0:T(8,128)(2,1)}, u32[]{:S(2)}) %copy-start) | copy-done | bytes 524312
  50.7 0.0 copy-start.1
  50.7 1.0 %copy-done.1 = bf16[64,3952]{1,0:T(8,128)(2,1)S(1)} copy-done((bf16[64,3952]{1,0:T(8,128)(2,1)S(1)}, bf16[64,3952]{1,0:T(8,128)(2,1)}, u32[]{:S(2)}) %copy-start.1) | copy-done | bytes 505880
  51.8 0.0 copy-start.2
  51.8 0.8 %copy-done.2 = f32[2,4096]{1,0:T(2,128)S(1)} copy-done((f32[2,4096]{1,0:T(2,128)S(1)}, f32[2,4096]{1,0:T(2,128)}, u32[]{:S(2)}) %copy-start.2) | copy-done | bytes 32792
  52.5 13.0 %head.1 = (bf16[3952,4096]{1,0:T(8,128)(2,1)}, bf16[2,4096]{1,0:T(2,128)(2,1)}) custom-call(bf16[64,3952]{1,0:T(8,128)(2,1)S(1)} %copy-done.1, bf16[64,4096]{1,0:T(8,128)(2,1)S(1)} %copy-done, f32[2,4096]{1,0:T(2,128)S(1)} %copy-done.2), custom_call_target="tpu_custom_call" | custom-call | flops 2071986176 | bytes 32374784 | tf_op jit(solution)/shard_map/head/pallas_call | solution.py:452
Async XLA Ops:
  49.7 1.0 %copy-start = (bf16[64,4096]{1,0:T(8,128)(2,1)S(1)}, bf16[64,4096]{1,0:T(8,128)(2,1)}, u32[]{:S(2)}) copy-start(bf16[64,4096]{1,0:T(8,128)(2,1)} %get-tuple-element.8.p_hbm) | copy-start | bytes 1572868
  50.7 1.0 %copy-start.1 = (bf16[64,3952]{1,0:T(8,128)(2,1)S(1)}, bf16[64,3952]{1,0:T(8,128)(2,1)}, u32[]{:S(2)}) copy-start(bf16[64,3952]{1,0:T(8,128)(2,1)} %get-tuple-element.7.g_hbm) | copy-start | bytes 1517572
  51.8 0.8 %copy-start.2 = (f32[2,4096]{1,0:T(2,128)S(1)}, f32[2,4096]{1,0:T(2,128)}, u32[]{:S(2)}) copy-start(f32[2,4096]{1,0:T(2,128)} %get-tuple-element.9.gh32_hbm) | copy-start | bytes 98308

commit v3 on v2

--- a/solution.py
+++ b/solution.py
@@ -24,7 +24,7 @@
     n_seq, n_voc, step,
     pos_ref, cnt_ref, hid_ref, tea_ref, w_hbm,
     picked_ref, grad_ref, gh_ref,
-    w_ref, gb, picked, stu, tex, grad, st1, st2, xs, xr, bs, br, cg, gh32,
+    w_ref, gb, picked, stu, tex, grad, exps, sums, st1, st2, xs, xr, bs, br, cg,
     w_sem, g1s, g1r, g2s, g2r, s1s, s1r, s2s, s2r, as_, ar, bss, bsr, cs, cr, out_sem,
 ):
     slots, vocab = tea_ref.shape
@@ -124,9 +124,15 @@
         lambda at, c: jnp.maximum(c, jnp.max(tea_ref[:, at].astype(F32), axis=1, keepdims=True)), low
     )
 
+    def split(i, at, e):
+        near = e.astype(BF16)
+        exps[i * slots : (i + 1) * slots, at] = near
+        exps[(i + 1) * slots : (i + 2) * slots, at] = (e - near.astype(F32)).astype(BF16)
+
     def teacher_total(at, c):
         e = jnp.exp(tea_ref[:, at].astype(F32) - top_t)
         tex[:, at] = e
+        split(2, at, e)
         return c + jnp.sum(e, axis=1, keepdims=True)
 
     tot_t = over(teacher_total, none)
@@ -176,6 +182,7 @@
     def student_total(at, c):
         e = jnp.exp(stu[:, at] - top_s)
         stu[:, at] = e
+        split(0, at, e)
         return c + jnp.sum(e, axis=1, keepdims=True)
 
     tot_s = over(student_total, none)
@@ -211,8 +218,36 @@
             jnp.sum(x[:, 4:5, :], axis=0),
         )
 
+    def half_of(i):
+        return (hv + 1 + i) % halves
+
+    def part(i, mine):
+        q = 2 * half_of(i) + (core if mine else other)
+
+        @pl.loop(0, 2)
+        def _(j):
+            at = pl.ds(pl.multiple_of(q * own_cols + j * sub, sub), sub)
+            out = jnp.dot(exps[...], w_ref[:, at], preferred_element_type=F32)
+            sums[0, 2 * i + mine, j] = out[0:slots] + out[slots : 2 * slots]
+            sums[1, 2 * i + mine, j] = out[2 * slots : 3 * slots] + out[3 * slots :]
+
+    def to_pair(i):
+        return pltpu.make_async_remote_copy(
+            src_ref=xs.at[i], dst_ref=xr.at[i], send_sem=as_.at[i], recv_sem=ar.at[i],
+            device_id=(s, pair), device_id_type=MESH,
+        )
+
+    def to_owner(i, k):
+        seq = (s + k) % n_seq
+        return pltpu.make_async_remote_copy(
+            src_ref=bs.at[i, seq], dst_ref=br.at[flat],
+            send_sem=bss.at[i, k], recv_sem=bsr.at[flat],
+            device_id=(seq, 2 * half_of(i) + core), device_id_type=MESH,
+        )
+
     for k in range(1, n_voc):
         stats1(k, v).start()
+    part(0, 0)
     for k in range(1, n_voc):
         stats1(k, (v + n_voc - k) % n_voc).wait_recv()
     slot_lane = lax.broadcasted_iota(jnp.int32, (1, lanes), 1)
@@ -224,6 +259,8 @@
     @pl.loop(1, n_seq)
     def _(k):
         stats2(k, s).start()
+
+    part(0, 1)
 
     @pl.loop(1, n_seq)
     def _(k):
@@ -238,57 +275,37 @@
     scale_s = cols[:, 1:2] * jnp.exp(top_s - cols[:, 0:1])
     scale_t = cols[:, 3:4] * jnp.exp(top_t - cols[:, 2:3])
 
+    def scaled(i, mine, j):
+        return scale_s * sums[0, 2 * i + mine, j] - scale_t * sums[1, 2 * i + mine, j]
+
+    def send_pair(i):
+        for j in range(2):
+            xs[i, j] = scaled(i, 0, j)
+        to_pair(i).start()
+
+    def send_owners(i):
+        to_pair(i).wait_recv()
+        both = [scaled(i, 1, j) + xr[i, j] for j in range(2)]
+        for q in range(n_seq):
+            rows_q = [x[q * cap : (q + 1) * cap] for x in both]
+            bs[i, q] = jnp.concatenate(rows_q, axis=0).astype(BF16)
+        for k in range(1 if i == halves - 1 else 0, n_seq):
+            to_owner(i, k).start()
+
     def logits(at, c):
         grad[:, at] = (scale_s * stu[:, at] - scale_t * tex[:, at]).astype(BF16)
         return c
 
+    send_pair(0)
+    grad_out = pltpu.make_async_copy(grad, grad_ref, out_sem.at[1])
     over(logits, 0)
-    grad_out = pltpu.make_async_copy(grad, grad_ref, out_sem.at[1])
     grad_out.start()
-
-    def part(q, store):
-        @pl.loop(0, 2)
-        def _(j):
-            at = pl.ds(pl.multiple_of(q * own_cols + j * sub, sub), sub)
-            store(j, jnp.dot(grad[...], w_ref[:, at], preferred_element_type=F32))
-
-    def to_pair(i):
-        return pltpu.make_async_remote_copy(
-            src_ref=xs.at[i], dst_ref=xr.at[i], send_sem=as_.at[i], recv_sem=ar.at[i],
-            device_id=(s, pair), device_id_type=MESH,
-        )
-
-    def to_owner(i, k):
-        h = (hv + 1 + i) % halves
-        seq = (s + k) % n_seq
-        return pltpu.make_async_remote_copy(
-            src_ref=bs.at[i, seq], dst_ref=br.at[flat],
-            send_sem=bss.at[i, k], recv_sem=bsr.at[flat],
-            device_id=(seq, 2 * h + core), device_id_type=MESH,
-        )
-
-    for i in range(halves):
-        h = (hv + 1 + i) % halves
-
-        def store_pair(j, value, i=i):
-            xs[i, j] = value
-
-        part(2 * h + other, store_pair)
-        to_pair(i).start()
-
-        def store_own(j, value, i=i):
-            for q in range(n_seq):
-                bs32 = value[q * cap : (q + 1) * cap]
-                gh32[q, pl.ds(pl.multiple_of(j * cap, cap), cap), :] = bs32
-
-        part(2 * h + core, store_own)
-        to_pair(i).wait_recv()
-        for q in range(n_seq):
-            for_q = [xr[i, j, q * cap : (q + 1) * cap, :] for j in range(2)]
-            bs[i, q] = (gh32[q] + jnp.concatenate(for_q, axis=0)).astype(BF16)
-        last = i == halves - 1
-        for k in range(1 if last else 0, n_seq):
-            to_owner(i, k).start()
+    for i in range(1, halves):
+        part(i, 0)
+        send_pair(i)
+        send_owners(i - 1)
+        part(i, 1)
+    send_owners(halves - 1)
 
     br[flat] = bs[halves - 1, s]
 
@@ -349,7 +366,7 @@
 
 
 def head_kernel(
-    step, g_hbm, p_hbm, gh32_hbm, out_hbm, gh_ref, g_ref, p_ref, gh32_ref, buf, sem, in_sem
+    step, g_hbm, p_hbm, gh32_hbm, out_hbm, gh_ref, g_ref, gt_ref, p_ref, gh32_ref, buf, sem, in_sem
 ):
     taken = [
         pltpu.make_async_copy(src, dst, in_sem.at[i])
@@ -363,10 +380,14 @@
     vocab = g_ref.shape[1]
     full, tail_at, tail = chunks_of(vocab, step)
 
+    def turn(at):
+        gt_ref[at, :] = g_ref[:, at].T
+
     def fill(at):
-        buf[at, :] = lax.dot_general(
-            g_ref[:, at], p_ref[...], (((0,), (0,)), ((), ())), preferred_element_type=F32
-        ).astype(BF16)
+        buf[at, :] = jnp.dot(gt_ref[at, :], p_ref[...], preferred_element_type=F32).astype(BF16)
+
+    def rows_of(i):
+        return pl.ds(pl.multiple_of(i * step, step), step)
 
     def copy(i):
         rows = pl.ds(pl.multiple_of(i * step, step), step)
@@ -379,10 +400,19 @@
         return pltpu.make_async_copy(buf.at[rows], out_hbm.at[rows], sem.at[full])
 
     if full:
-        @pl.loop(0, full)
+        turn(rows_of(0))
+
+        @pl.loop(0, full - 1)
         def _(i):
-            fill(pl.ds(pl.multiple_of(i * step, step), step))
+            turn(rows_of(i + 1))
+            fill(rows_of(i))
             copy(i).start()
+
+    if tail:
+        turn(pl.ds(tail_at, tail))
+    if full:
+        fill(rows_of(full - 1))
+        copy(full - 1).start()
     if tail:
         fill(pl.ds(tail_at, tail))
         copy_tail().start()
@@ -424,6 +454,8 @@
             pltpu.VMEM((slots, vocab), F32),
             pltpu.VMEM((slots, vocab), F32),
             pltpu.VMEM((slots, vocab), BF16),
+            pltpu.VMEM((4 * slots, vocab), BF16),
+            pltpu.VMEM((2, n_voc, 2, slots, sub), F32),
             pltpu.VMEM((n_voc, 8, lanes), F32),
             pltpu.VMEM((n_seq, 8, lanes), F32),
             pltpu.VMEM((halves, 2, slots, sub), F32),
@@ -431,7 +463,6 @@
             pltpu.VMEM((halves, n_seq, 2 * cap, sub), BF16),
             pltpu.VMEM((group, 2 * cap, sub), BF16),
             pltpu.VMEM((n_voc, 2 * cap, sub), BF16),
-            pltpu.VMEM((n_seq, 2 * cap, sub), F32),
             dma((n_chunks,)),
             dma((n_seq,)), dma((n_seq,)), dma((n_seq,)), dma((n_seq,)),
             dma((n_voc,)), dma((n_voc,)), dma((n_seq,)), dma((n_seq,)),
@@ -455,17 +486,18 @@
             jax.ShapeDtypeStruct((vocab, depth), BF16),
             jax.ShapeDtypeStruct((cap // n_voc, depth), BF16),
         ),
-        in_specs=[anywhere, anywhere, anywhere],
+        in_specs=[pl.BlockSpec(memory_space=pltpu.HBM)] * 3,
         out_specs=(anywhere, vmem),
         scratch_shapes=[
             pltpu.VMEM((slots, vocab), BF16),
+            pltpu.VMEM((vocab, slots), BF16),
             pltpu.VMEM((slots, depth), BF16),
             pltpu.VMEM((cap // n_voc, depth), F32),
             pltpu.VMEM((vocab, depth), BF16),
             dma((chunks_of(vocab, rows)[0] + 1,)),
             dma((3,)),
         ],
-        compiler_params=pltpu.CompilerParams(vmem_limit_bytes=48 * 1024 * 1024),
+        compiler_params=pltpu.CompilerParams(vmem_limit_bytes=60 * 1024 * 1024),
         cost_estimate=pl.CostEstimate(
             flops=2 * slots * depth * vocab, bytes_accessed=2 * depth * vocab, transcendentals=0
         ),

time: 65.8 us -> 62.7 us (0.953)
  local copies, waits for them, and re-layouts: 2.83 us -> 0 us
    unnamed x6 -> x0, local copies, waits for them, and re-layouts: 2.83 us -> none
    pallas_call x1, Pallas kernels: 48.4 us -> 47.2 us  [per_device(): pl.pallas_call(functools.partial(front_kernel, n_seq, n_voc, step), out_s...]
    pallas_call x1, Pallas kernels: 13 us -> 14 us  [per_device(): pl.pallas_call(functools.partial(head_kernel, rows), out_shape=(jax.Shape...]
where the time goes in v3:
time: 62.7 us; the launch traced here: 62.5 us
  Pallas kernels  61.2 us (98%)
  between operations  1.29 us (2%)
    pallas_call x1, Pallas kernels, per_device(): pl.pallas_call(functools.partial(front_kernel, n_seq, n_voc, step), out_s...  47.2 us
    pallas_call x1, Pallas kernels, per_device(): pl.pallas_call(functools.partial(head_kernel, rows), out_shape=(jax.Shape...  14 us

profile of v3, /device:TPU:0, one launch (start us, length us, event | category | flops | bytes accessed | tf_op | source)
XLA Modules:
  0.0 62.5 jit_solution(13036318616783306106)
XLA Ops:
  1.3 47.2 %front.1 = (bf16[64,4096]{1,0:T(8,128)(2,1)}, bf16[64,3952]{1,0:T(8,128)(2,1)}, f32[2,4096]{1,0:T(2,128)}) custom-call(s32[1,8]{1,0:T(1,128)} %pos_ref.1, s32[1]{0:T(128)S(6)} %copy.7.cnt_ref, bf16[64,4096]{1,0:T(8,128)(2,1)} %hid_ref.1, bf16[64,3952]{1,0:T(8,128)(2,1)} %tea_ref.1, bf16[3952,4096]{1,0:T(8,128)(2,1)} %bitcast.2), custom_call_target="tpu_custom_call" | custom-call | flops 4143972352 | bytes 32374784 | tf_op jit(solution)/shard_map/front/pallas_call | solution.py:441
  48.5 14.0 %head.1 = (bf16[3952,4096]{1,0:T(8,128)(2,1)}, bf16[2,4096]{1,0:T(2,128)(2,1)}) custom-call(bf16[64,3952]{1,0:T(8,128)(2,1)} %get-tuple-element.7.g_hbm, bf16[64,4096]{1,0:T(8,128)(2,1)} %get-tuple-element.8.p_hbm, f32[2,4096]{1,0:T(2,128)} %get-tuple-element.9.gh32_hbm), custom_call_target="tpu_custom_call" | custom-call | flops 2071986176 | bytes 32374784 | tf_op jit(solution)/shard_map/head/pallas_call | solution.py:483

commit v4 on v3

--- a/solution.py
+++ b/solution.py
@@ -297,15 +297,16 @@
         return c
 
     send_pair(0)
-    grad_out = pltpu.make_async_copy(grad, grad_ref, out_sem.at[1])
-    over(logits, 0)
-    grad_out.start()
     for i in range(1, halves):
         part(i, 0)
         send_pair(i)
         send_owners(i - 1)
         part(i, 1)
     send_owners(halves - 1)
+
+    over(logits, 0)
+    grad_out = pltpu.make_async_copy(grad, grad_ref, out_sem.at[1])
+    grad_out.start()
 
     br[flat] = bs[halves - 1, s]
 
@@ -479,7 +480,7 @@
         name="front",
     )(positions, counts, hidden, teacher, head_weight.T)
 
-    rows = 512
+    rows = 256
     head, gh = pl.pallas_call(
         functools.partial(head_kernel, rows),
         out_shape=(

time: 62.7 us -> 63.3 us (level)
    pallas_call x1, Pallas kernels: 14 us -> 14.7 us  [per_device(): pl.pallas_call(functools.partial(head_kernel, rows), out_shape=(jax.Shape...]
where the time goes in v4:
time: 63.3 us; the launch traced here: 63.1 us
  Pallas kernels  61.8 us (98%)
  between operations  1.29 us (2%)
    pallas_call x1, Pallas kernels, per_device(): pl.pallas_call(functools.partial(front_kernel, n_seq, n_voc, step), out_s...  47.1 us
    pallas_call x1, Pallas kernels, per_device(): pl.pallas_call(functools.partial(head_kernel, rows), out_shape=(jax.Shape...  14.7 us

profile of v4, /device:TPU:0, one launch (start us, length us, event | category | flops | bytes accessed | tf_op | source)
XLA Modules:
  0.0 63.1 jit_solution(17032919213198874751)
XLA Ops:
  1.3 47.1 %front.1 = (bf16[64,4096]{1,0:T(8,128)(2,1)}, bf16[64,3952]{1,0:T(8,128)(2,1)}, f32[2,4096]{1,0:T(2,128)}) custom-call(s32[1,8]{1,0:T(1,128)} %pos_ref.1, s32[1]{0:T(128)S(6)} %copy.7.cnt_ref, bf16[64,4096]{1,0:T(8,128)(2,1)} %hid_ref.1, bf16[64,3952]{1,0:T(8,128)(2,1)} %tea_ref.1, bf16[3952,4096]{1,0:T(8,128)(2,1)} %bitcast.2), custom_call_target="tpu_custom_call" | custom-call | flops 4143972352 | bytes 32374784 | tf_op jit(solution)/shard_map/front/pallas_call | solution.py:442
  48.4 14.7 %head.1 = (bf16[3952,4096]{1,0:T(8,128)(2,1)}, bf16[2,4096]{1,0:T(2,128)(2,1)}) custom-call(bf16[64,3952]{1,0:T(8,128)(2,1)} %get-tuple-element.7.g_hbm, bf16[64,4096]{1,0:T(8,128)(2,1)} %get-tuple-element.8.p_hbm, f32[2,4096]{1,0:T(2,128)} %get-tuple-element.9.gh32_hbm), custom_call_target="tpu_custom_call" | custom-call | flops 2071986176 | bytes 32374784 | tf_op jit(solution)/shard_map/head/pallas_call | solution.py:484
